TPU v7x, 32 devices: a whole 2x2x4 slice. The times are simulated.
32 devices in a mesh: parts: 2 (over x), seq: 16 (over z, y, core).
Axes of the slice: x: 2, y: 2, z: 4, core: 2. Of those that a mesh axis runs over, the one named last changes fastest.
Arguments:
- queries: bfloat16 [6144, 8, 128], P(('parts', 'seq')), parts along dimension 0, may hold values from -6 to 6
- key_rows: bfloat16 [6144, 8, 128], P(('parts', 'seq')), parts along dimension 0, may hold values from -6 to 6
- value_rows: bfloat16 [6144, 8, 128], P(('parts', 'seq')), parts along dimension 0, may hold values from -6 to 6
- grad_out: bfloat16 [6144, 8, 128], P(('parts', 'seq')), parts along dimension 0, may hold values from -6 to 6
- kv_tiles: int32 [96, 12], P('parts'), parts along dimension 0, may hold values from 0 to 47, as said below
- counts: int32 [96], P('parts'), parts along dimension 0, may hold values from 4 to 12, as said below
Outputs:
- attended: bfloat16 [6144, 8, 128], P(('parts', 'seq')), parts along dimension 0
- grad_queries: bfloat16 [6144, 8, 128], P(('parts', 'seq')), parts along dimension 0
- grad_keys: bfloat16 [6144, 8, 128], P(('parts', 'seq')), parts along dimension 0
- grad_values: bfloat16 [6144, 8, 128], P(('parts', 'seq')), parts along dimension 0
There are 2 independent parts, one for each index of `parts`. A program takes and returns all parts, laid end to end along the dimension named above; each array names one. Nothing has to cross between parts.
Inputs may be any that keep to these rules, and one draw needn't show every extreme that they name: `kv_tiles`: tiles form frames of 4 rows of 3 tiles each, in order frame, row, column. Row i holds distinct tiles that differ from tile i by at most one in frame, row and column, the first being i itself, in its first counts[i] entries; the remaining entries equal i. counts[i] is at most the number of tiles within one frame, row and column of tile i; some tile has exactly 12.
All inputs are finite; a program needn't handle non-finite values.
Results may differ from a plain program's by a relative error of at most 0.018.
Values may be sent and summed in bfloat16 or wider, within the bound.
A program may use at most 128 MiB of HBM per device.

v0:
```python
import jax
import jax.numpy as jnp
from jax import lax
from jax.sharding import PartitionSpec as P

TILE = 64


BAND_OFFSETS = (-5, -4, -3, -1, 0, 1, 3, 4, 5)


def passed_along(value, axis, steps):
    count = lax.axis_size(axis)
    first, last = (max(0, -steps), min(count, count - steps))
    return lax.ppermute(value, axis, [(source, source + steps) for source in range(first, last)])


def band_position(offsets):
    position = jnp.zeros_like(offsets)
    for slot_place, band_step in enumerate(BAND_OFFSETS):
        position = position + jnp.where(offsets == band_step, slot_place, 0)
    return position


def on_device(queries, key_rows, value_rows, grad_out, kv_tiles, counts):
    tok_dev, heads, head_dim = queries.shape
    tiles_dev = tok_dev // TILE
    list_len = kv_tiles.shape[1]
    band_tiles = len(BAND_OFFSETS) * tiles_dev
    row_width = TILE * heads * head_dim
    scale_qk = head_dim ** (-0.5)
    device = lax.axis_index("seq")
    first_tile = device * tiles_dev
    my_lists = lax.dynamic_slice_in_dim(kv_tiles, first_tile, tiles_dev, 0)
    my_counts = lax.dynamic_slice_in_dim(counts, first_tile, tiles_dev, 0)
    stacked = jnp.stack([key_rows, value_rows])
    blocks = []
    for offset in BAND_OFFSETS:
        if offset == 0:
            blocks.append(stacked)
        else:
            blocks.append(passed_along(stacked, "seq", -offset))
    bank = jnp.concatenate(blocks, axis=1)
    bank = bank.reshape(2, band_tiles, TILE, heads, head_dim)
    owner_offset = my_lists // tiles_dev - device
    slots = band_position(owner_offset) * tiles_dev + my_lists % tiles_dev
    valid = jnp.arange(list_len)[None, :] < my_counts[:, None]
    query_tiles = queries.reshape(tiles_dev, TILE, heads, head_dim)
    grad_tiles = grad_out.reshape(tiles_dev, TILE, heads, head_dim)

    def one_tile(bank_acc, inputs):
        query_one, grad_one, slot_row, valid_row = inputs
        picked = jnp.take(bank, slot_row, axis=1).reshape(2, list_len * TILE, heads, head_dim)
        keys_sel = picked[0]
        values_sel = picked[1]
        key_mask = jnp.repeat(valid_row, TILE)
        scores = (
            jnp.einsum("qhd,khd->hqk", query_one, keys_sel, preferred_element_type=jnp.float32)
            * scale_qk
        )
        scores = jnp.where(key_mask[None, None, :], scores, -jnp.inf)
        row_max = jnp.max(scores, axis=-1, keepdims=True)
        log_total = row_max + jnp.log(jnp.sum(jnp.exp(scores - row_max), axis=-1, keepdims=True))
        weights = jnp.exp(scores - log_total).astype(jnp.bfloat16)
        attended_one = jnp.einsum(
            "hqk,khd->qhd", weights, values_sel, preferred_element_type=jnp.float32
        ).astype(jnp.bfloat16)
        grad_weights = jnp.einsum(
            "qhd,khd->hqk", grad_one, values_sel, preferred_element_type=jnp.float32
        )
        delta = jnp.transpose(
            jnp.sum(grad_one.astype(jnp.float32) * attended_one.astype(jnp.float32), axis=-1)
        )
        grad_scores = (
            weights.astype(jnp.float32) * (grad_weights - delta[:, :, None]) * scale_qk
        ).astype(jnp.bfloat16)
        grad_query = jnp.einsum(
            "hqk,khd->qhd", grad_scores, keys_sel, preferred_element_type=jnp.float32
        ).astype(jnp.bfloat16)
        part_keys = jnp.einsum(
            "hqk,qhd->khd", grad_scores, query_one, preferred_element_type=jnp.float32
        )
        part_values = jnp.einsum(
            "hqk,qhd->khd", weights, grad_one, preferred_element_type=jnp.float32
        )
        parts_both = jnp.stack([part_keys, part_values]).reshape(2, list_len, row_width)
        bank_acc = bank_acc.at[:, slot_row].add(parts_both)
        return (bank_acc, (attended_one, grad_query, log_total[:, :, 0], delta))

    bank_init = jnp.zeros((2, band_tiles, row_width), jnp.float32)
    bank_grad, (attended_t, grad_query_t, log_tiles, delta_tiles) = lax.scan(
        one_tile, bank_init, (query_tiles, grad_tiles, slots, valid)
    )
    attended = attended_t.reshape(tok_dev, heads, head_dim)
    grad_queries = grad_query_t.reshape(tok_dev, heads, head_dim)
    bank_grad = bank_grad.reshape(2, len(BAND_OFFSETS), tok_dev, heads, head_dim)
    totals = bank_grad[:, BAND_OFFSETS.index(0)]
    for slot_place, offset in enumerate(BAND_OFFSETS):
        if offset != 0:
            totals = totals + passed_along(bank_grad[:, slot_place], "seq", offset)
    grad_keys = totals[0].astype(jnp.bfloat16)
    grad_values = totals[1].astype(jnp.bfloat16)
    return (attended, grad_queries, grad_keys, grad_values)


def solution(mesh):
    return jax.shard_map(
        on_device,
        mesh=mesh,
        in_specs=(
            P(("parts", "seq"), None, None),
            P(("parts", "seq"), None, None),
            P(("parts", "seq"), None, None),
            P(("parts", "seq"), None, None),
            P("parts", None),
            P("parts"),
        ),
        out_specs=(
            P(("parts", "seq"), None, None),
            P(("parts", "seq"), None, None),
            P(("parts", "seq"), None, None),
            P(("parts", "seq"), None, None),
        ),
        check_vma=False,
    )
```

profile of v0, /device:TPU:22, one launch (start us, length us, event | category | flops | bytes accessed | tf_op | source)
XLA Modules:
  0.0 531.3 jit_solution(10653839417177516762)
XLA Ops:
  14.6 13.8 %collective-permute-done = bf16[2,192,8,128]{3,2,1,0:T(8,128)(2,1)} collective-permute-done((bf16[2,192,8,128]{3,2,1,0:T(8,128)(2,1)S(1)}, bf16[2,192,8,128]{3,2,1,0:T(8,128)(2,1)}, u32[]{:S(2)}, u32[]{:S(2)}) %collective-permute-start) | collective-permute-done | bytes 786464 | tf_op jit(solution)/shard_map/ppermute | solution.py:15
  28.4 5.7 %collective-permute-start.5 = (bf16[2,192,8,128]{3,2,1,0:T(8,128)(2,1)S(1)}, bf16[2,192,8,128]{3,2,1,0:T(8,128)(2,1)S(1)}, u32[]{:S(2)}, u32[]{:S(2)}) collective-permute-start(bf16[2,192,8,128]{3,2,1,0:T(8,128)(2,1)S(1)} %pad_maximum_fusion), channel_id=1, source_target_pairs={{3,0},{4,1},{5,2},{6,3},{7,4},{8,5},{9,6},{10,7},{11,8},{12,9},{13... | collective-permute-start | bytes 2359304 | tf_op jit(solution)/shard_map/ppermute | solution.py:15
  36.3 11.6 %collective-permute-done.1 = bf16[2,192,8,128]{3,2,1,0:T(8,128)(2,1)S(1)} collective-permute-done((bf16[2,192,8,128]{3,2,1,0:T(8,128)(2,1)S(1)}, bf16[2,192,8,128]{3,2,1,0:T(8,128)(2,1)S(1)}, u32[]{:S(2)}, u32[]{:S(2)}) %collective-permute-start.1) | collective-permute-done | bytes 786464 | tf_op jit(solution)/shard_map/ppermute | solution.py:15
  50.9 23.4 %collective-permute-done.2 = bf16[2,192,8,128]{3,2,1,0:T(8,128)(2,1)} collective-permute-done((bf16[2,192,8,128]{3,2,1,0:T(8,128)(2,1)S(1)}, bf16[2,192,8,128]{3,2,1,0:T(8,128)(2,1)}, u32[]{:S(2)}, u32[]{:S(2)}) %collective-permute-start.2) | collective-permute-done | bytes 786464 | tf_op jit(solution)/shard_map/ppermute | solution.py:15
  83.2 4.6 collective-permute-done.7
  88.7 5.2 broadcast_in_dim.75
  93.8 221.3 %while.14 = (s32[]{:T(128)}, f32[2,27,65536]{2,0,1:T(2,128)}, bf16[3,64,8,128]{3,2,1,0:T(8,128)(2,1)}, bf16[3,64,8,128]{3,2,1,0:T(8,128)(2,1)}, s32[3,12]{1,0:T(...) while((s32[]{:T(128)}, f32[2,27,65536]{2,0,1:T(2,128)}, ...), condition=%wide.region_5.6_spmd, body=%wide.region_0.5_spmd.sunk | while | flops 613810304 | bytes 122316280 | solution.py:91
  121.6 7.2 %maximum_bitcast_fusion.2 = f32[12,2,65536]{2,0,1:T(8,128)} fusion(f32[1,12,65536]{2,1,0:T(8,128)} %stack.23, f32[1,12,65536]{2,1,0:T(8,128)} %stack.24), kind=kLoop, calls=%fused_computation.2.clone.1 | loop fusion | flops 1572864 | bytes 12582912 | tf_op jit(solution)/shard_map/while/body/eval_jaxpr/stack | solution.py:86
  128.9 10.9 %copy.82 = f32[12,2,65536]{2,1,0:T(2,128)} copy(f32[12,2,65536]{2,0,1:T(8,128)} %maximum_bitcast_fusion.2) | data formatting | bytes 12582912 | tf_op jit(solution)/shard_map/while/body/eval_jaxpr/stack | solution.py:86
  139.8 28.0 %scatter_fusion = f32[2,27,65536]{2,0,1:T(2,128)} fusion(f32[2,27,65536]{2,0,1:T(2,128)} %get-tuple-element.183, s32[12]{0:T(128)S(1)} %fusion.44, f32[12,2,65536]{2,1,0:T(2,128)} %copy.82), kind=kCustom, calls=%fused_computation.1.clone.1 | custom fusion | flops 1572864 | bytes 18874416 | tf_op jit(solution)/shard_map/while/body/eval_jaxpr/scatter-add | solution.py:87
  195.5 7.2 %maximum_bitcast_fusion.2 = f32[12,2,65536]{2,0,1:T(8,128)} fusion(f32[1,12,65536]{2,1,0:T(8,128)} %stack.23, f32[1,12,65536]{2,1,0:T(8,128)} %stack.24), kind=kLoop, calls=%fused_computation.2.clone.1 | loop fusion | flops 1572864 | bytes 12582912 | tf_op jit(solution)/shard_map/while/body/eval_jaxpr/stack | solution.py:86
  202.7 10.9 %copy.82 = f32[12,2,65536]{2,1,0:T(2,128)} copy(f32[12,2,65536]{2,0,1:T(8,128)} %maximum_bitcast_fusion.2) | data formatting | bytes 12582912 | tf_op jit(solution)/shard_map/while/body/eval_jaxpr/stack | solution.py:86
  213.6 27.7 %scatter_fusion = f32[2,27,65536]{2,0,1:T(2,128)} fusion(f32[2,27,65536]{2,0,1:T(2,128)} %get-tuple-element.183, s32[12]{0:T(128)S(1)} %fusion.44, f32[12,2,65536]{2,1,0:T(2,128)} %copy.82), kind=kCustom, calls=%fused_computation.1.clone.1 | custom fusion | flops 1572864 | bytes 18874416 | tf_op jit(solution)/shard_map/while/body/eval_jaxpr/scatter-add | solution.py:87
  269.1 7.2 %maximum_bitcast_fusion.2 = f32[12,2,65536]{2,0,1:T(8,128)} fusion(f32[1,12,65536]{2,1,0:T(8,128)} %stack.23, f32[1,12,65536]{2,1,0:T(8,128)} %stack.24), kind=kLoop, calls=%fused_computation.2.clone.1 | loop fusion | flops 1572864 | bytes 12582912 | tf_op jit(solution)/shard_map/while/body/eval_jaxpr/stack | solution.py:86
  276.3 10.9 %copy.82 = f32[12,2,65536]{2,1,0:T(2,128)} copy(f32[12,2,65536]{2,0,1:T(8,128)} %maximum_bitcast_fusion.2) | data formatting | bytes 12582912 | tf_op jit(solution)/shard_map/while/body/eval_jaxpr/stack | solution.py:86
  287.2 27.9 %scatter_fusion = f32[2,27,65536]{2,0,1:T(2,128)} fusion(f32[2,27,65536]{2,0,1:T(2,128)} %get-tuple-element.183, s32[12]{0:T(128)S(1)} %fusion.44, f32[12,2,65536]{2,1,0:T(2,128)} %copy.82), kind=kCustom, calls=%fused_computation.1.clone.1 | custom fusion | flops 1572864 | bytes 18874416 | tf_op jit(solution)/shard_map/while/body/eval_jaxpr/scatter-add | solution.py:87
  315.1 19.0 %copy.25 = f32[2,27,65536]{2,1,0:T(8,128)} copy(f32[2,27,65536]{2,0,1:T(2,128)} %get-tuple-element.55) | data formatting | bytes 28311552 | tf_op jit(solution)/shard_map/while | solution.py:91
  334.1 15.2 %reshape.90 = f32[2,9,192,8,128]{4,3,2,1,0:T(8,128)} reshape(f32[2,27,65536]{2,1,0:T(8,128)} %copy.25) | data formatting | bytes 28311552 | tf_op jit(solution)/shard_map/reshape | solution.py:96
  349.3 7.6 %slice_bitcast_fusion.7 = (f32[2,192,8,128]{3,2,1,0:T(8,128)}, f32[2,192,8,128]{3,2,1,0:T(8,128)}, f32[2,192,8,128]{3,2,1,0:T(8,128)}, f32[2,192,8,128]{3,2,1,0:...) fusion(f32[2,9,192,8,128]{4,3,2,1,0:T(8,128)} %reshape.90), kind=kLoop, calls=%fused_computation.35 | loop fusion | bytes 25165824 | tf_op jit(solution)/shard_map/squeeze | solution.py:100
  359.7 8.4 %collective-permute-start.13 = (f32[2,192,8,128]{3,2,1,0:T(8,128)}, f32[2,192,8,128]{3,2,1,0:T(8,128)S(1)}, u32[]{:S(2)}, u32[]{:S(2)}) collective-permute-start(f32[2,192,8,128]{3,2,1,0:T(8,128)} %get-tuple-element.92), channel_id=1, source_target_pairs={{0,3},{1,4},{2,5},{3,6},{4,7},{5,8},{6,9},{7,10},{8,11},{9,12},{10... | collective-permute-start | bytes 4718600 | tf_op jit(solution)/shard_map/ppermute | solution.py:15
  377.6 17.2 %collective-permute-done.8 = f32[2,192,8,128]{3,2,1,0:T(8,128)S(1)} collective-permute-done((f32[2,192,8,128]{3,2,1,0:T(8,128)}, f32[2,192,8,128]{3,2,1,0:T(8,128)S(1)}, u32[]{:S(2)}, u32[]{:S(2)}) %collective-permute-start.8) | collective-permute-done | bytes 1572896 | tf_op jit(solution)/shard_map/ppermute | solution.py:15
  396.7 6.6 %collective-permute-done.13 = f32[2,192,8,128]{3,2,1,0:T(8,128)S(1)} collective-permute-done((f32[2,192,8,128]{3,2,1,0:T(8,128)}, f32[2,192,8,128]{3,2,1,0:T(8,128)S(1)}, u32[]{:S(2)}, u32[]{:S(2)}) %collective-permute-start.13) | collective-permute-done | bytes 1572896 | tf_op jit(solution)/shard_map/ppermute | solution.py:15
  405.2 51.4 %collective-permute-done.12 = f32[2,192,8,128]{3,2,1,0:T(8,128)S(1)} collective-permute-done((f32[2,192,8,128]{3,2,1,0:T(8,128)}, f32[2,192,8,128]{3,2,1,0:T(8,128)S(1)}, u32[]{:S(2)}, u32[]{:S(2)}) %collective-permute-start.12) | collective-permute-done | bytes 1572896 | tf_op jit(solution)/shard_map/ppermute | solution.py:15
  458.6 69.5 %collective-permute-done.14 = f32[2,192,8,128]{3,2,1,0:T(8,128)S(1)} collective-permute-done((f32[2,192,8,128]{3,2,1,0:T(8,128)S(1)}, f32[2,192,8,128]{3,2,1,0:T(8,128)S(1)}, u32[]{:S(2)}, u32[]{:S(2)}) %collective-permute-start.14) | collective-permute-done | bytes 1572896 | tf_op jit(solution)/shard_map/ppermute | solution.py:15
  (138 shorter events, 132.9 us)
Async XLA Ops:
  0.6 13.7 %copy-start = (s32[48,12]{0,1:T(8,128)S(1)}, s32[48,12]{0,1:T(8,128)}, u32[]{:S(2)}) copy-start(s32[48,12]{0,1:T(8,128)} %param.12) | copy-start | bytes 6916
  0.6 13.6 %copy-start.5 = (s32[48]{0:T(128)S(1)}, s32[48]{0:T(128)}, u32[]{:S(2)}) copy-start(s32[48]{0:T(128)} %param.13) | copy-start | bytes 580
  1.9 26.6 %collective-permute-start = (bf16[2,192,8,128]{3,2,1,0:T(8,128)(2,1)S(1)}, bf16[2,192,8,128]{3,2,1,0:T(8,128)(2,1)}, u32[]{:S(2)}, u32[]{:S(2)}) collective-permute-start(bf16[2,192,8,128]{3,2,1,0:T(8,128)(2,1)S(1)} %pad_maximum_fusion), channel_id=1, source_target_pairs={{0,5},{1,6},{2,7},{3,8},{4,9},{5,10},{6,11},{7,12},{8,13},{9,14},{... | collective-permute-start | bytes 2359304 | tf_op jit(solution)/shard_map/ppermute | solution.py:15
  4.8 43.2 %collective-permute-start.1 = (bf16[2,192,8,128]{3,2,1,0:T(8,128)(2,1)S(1)}, bf16[2,192,8,128]{3,2,1,0:T(8,128)(2,1)S(1)}, u32[]{:S(2)}, u32[]{:S(2)}) collective-permute-start(bf16[2,192,8,128]{3,2,1,0:T(8,128)(2,1)S(1)} %pad_maximum_fusion), channel_id=1, source_target_pairs={{0,4},{1,5},{2,6},{3,7},{4,8},{5,9},{6,10},{7,11},{8,12},{9,13},{1... | collective-permute-start | bytes 2359304 | tf_op jit(solution)/shard_map/ppermute | solution.py:15
  6.7 73.6 %collective-permute-start.4 = (bf16[2,192,8,128]{3,2,1,0:T(8,128)(2,1)S(1)}, bf16[2,192,8,128]{3,2,1,0:T(8,128)(2,1)S(1)}, u32[]{:S(2)}, u32[]{:S(2)}) collective-permute-start(bf16[2,192,8,128]{3,2,1,0:T(8,128)(2,1)S(1)} %pad_maximum_fusion), channel_id=1, source_target_pairs={{1,0},{2,1},{3,2},{4,3},{5,4},{6,5},{7,6},{8,7},{9,8},{10,9},{11,1... | collective-permute-start | bytes 2359304 | tf_op jit(solution)/shard_map/ppermute | solution.py:15
  10.4 68.0 %collective-permute-start.3 = (bf16[2,192,8,128]{3,2,1,0:T(8,128)(2,1)S(1)}, bf16[2,192,8,128]{3,2,1,0:T(8,128)(2,1)S(1)}, u32[]{:S(2)}, u32[]{:S(2)}) collective-permute-start(bf16[2,192,8,128]{3,2,1,0:T(8,128)(2,1)S(1)} %pad_maximum_fusion), channel_id=1, source_target_pairs={{0,1},{1,2},{2,3},{3,4},{4,5},{5,6},{6,7},{7,8},{8,9},{9,10},{10,1... | collective-permute-start | bytes 2359304 | tf_op jit(solution)/shard_map/ppermute | solution.py:15
  12.3 62.0 %collective-permute-start.2 = (bf16[2,192,8,128]{3,2,1,0:T(8,128)(2,1)S(1)}, bf16[2,192,8,128]{3,2,1,0:T(8,128)(2,1)}, u32[]{:S(2)}, u32[]{:S(2)}) collective-permute-start(bf16[2,192,8,128]{3,2,1,0:T(8,128)(2,1)S(1)} %pad_maximum_fusion), channel_id=1, source_target_pairs={{0,3},{1,4},{2,5},{3,6},{4,7},{5,8},{6,9},{7,10},{8,11},{9,12},{10... | collective-permute-start | bytes 2359304 | tf_op jit(solution)/shard_map/ppermute | solution.py:15
  28.4 52.8 %collective-permute-start.5 = (bf16[2,192,8,128]{3,2,1,0:T(8,128)(2,1)S(1)}, bf16[2,192,8,128]{3,2,1,0:T(8,128)(2,1)S(1)}, u32[]{:S(2)}, u32[]{:S(2)}) collective-permute-start(bf16[2,192,8,128]{3,2,1,0:T(8,128)(2,1)S(1)} %pad_maximum_fusion), channel_id=1, source_target_pairs={{3,0},{4,1},{5,2},{6,3},{7,4},{8,5},{9,6},{10,7},{11,8},{12,9},{13... | collective-permute-start | bytes 2359304 | tf_op jit(solution)/shard_map/ppermute | solution.py:15
  48.0 34.3 %collective-permute-start.6 = (bf16[2,192,8,128]{3,2,1,0:T(8,128)(2,1)S(1)}, bf16[2,192,8,128]{3,2,1,0:T(8,128)(2,1)S(1)}, u32[]{:S(2)}, u32[]{:S(2)}) collective-permute-start(bf16[2,192,8,128]{3,2,1,0:T(8,128)(2,1)S(1)} %pad_maximum_fusion), channel_id=1, source_target_pairs={{4,0},{5,1},{6,2},{7,3},{8,4},{9,5},{10,6},{11,7},{12,8},{13,9},{1... | collective-permute-start | bytes 2359304 | tf_op jit(solution)/shard_map/ppermute | solution.py:15
  50.9 28.5 %copy-start.3 = (bf16[192,8,128]{2,1,0:T(8,128)(2,1)S(1)}, bf16[192,8,128]{2,1,0:T(8,128)(2,1)}, u32[]{:S(2)}) copy-start(bf16[192,8,128]{2,1,0:T(8,128)(2,1)} %param.10) | copy-start | bytes 1179652
  50.9 28.5 %copy-start.4 = (bf16[192,8,128]{2,1,0:T(8,128)(2,1)S(1)}, bf16[192,8,128]{2,1,0:T(8,128)(2,1)}, u32[]{:S(2)}) copy-start(bf16[192,8,128]{2,1,0:T(8,128)(2,1)} %param.9) | copy-start | bytes 1179652
  74.3 13.5 %collective-permute-start.7 = (bf16[2,192,8,128]{3,2,1,0:T(8,128)(2,1)S(1)}, bf16[2,192,8,128]{3,2,1,0:T(8,128)(2,1)S(1)}, u32[]{:S(2)}, u32[]{:S(2)}) collective-permute-start(bf16[2,192,8,128]{3,2,1,0:T(8,128)(2,1)S(1)} %pad_maximum_fusion), channel_id=1, source_target_pairs={{5,0},{6,1},{7,2},{8,3},{9,4},{10,5},{11,6},{12,7},{13,8},{14,9},{... | collective-permute-start | bytes 2359304 | tf_op jit(solution)/shard_map/ppermute | solution.py:15
  103.1 1.2 copy-start.2
  177.0 1.2 copy-start.2
  250.6 1.2 copy-start.2
  356.9 37.9 %collective-permute-start.8 = (f32[2,192,8,128]{3,2,1,0:T(8,128)}, f32[2,192,8,128]{3,2,1,0:T(8,128)S(1)}, u32[]{:S(2)}, u32[]{:S(2)}) collective-permute-start(f32[2,192,8,128]{3,2,1,0:T(8,128)} %get-tuple-element.91), channel_id=1, source_target_pairs={{5,0},{6,1},{7,2},{8,3},{9,4},{10,5},{11,6},{12,7},{13,8},{14,9},{... | collective-permute-start | bytes 4718600 | tf_op jit(solution)/shard_map/ppermute | solution.py:15
  359.7 43.6 %collective-permute-start.13 = (f32[2,192,8,128]{3,2,1,0:T(8,128)}, f32[2,192,8,128]{3,2,1,0:T(8,128)S(1)}, u32[]{:S(2)}, u32[]{:S(2)}) collective-permute-start(f32[2,192,8,128]{3,2,1,0:T(8,128)} %get-tuple-element.92), channel_id=1, source_target_pairs={{0,3},{1,4},{2,5},{3,6},{4,7},{5,8},{6,9},{7,10},{8,11},{9,12},{10... | collective-permute-start | bytes 4718600 | tf_op jit(solution)/shard_map/ppermute | solution.py:15
  368.1 88.5 %collective-permute-start.12 = (f32[2,192,8,128]{3,2,1,0:T(8,128)}, f32[2,192,8,128]{3,2,1,0:T(8,128)S(1)}, u32[]{:S(2)}, u32[]{:S(2)}) collective-permute-start(f32[2,192,8,128]{3,2,1,0:T(8,128)} %get-tuple-element.93), channel_id=1, source_target_pairs={{0,1},{1,2},{2,3},{3,4},{4,5},{5,6},{6,7},{7,8},{8,9},{9,10},{10,1... | collective-permute-start | bytes 4718600 | tf_op jit(solution)/shard_map/ppermute | solution.py:15
  370.1 88.5 %collective-permute-start.11 = (f32[2,192,8,128]{3,2,1,0:T(8,128)}, f32[2,192,8,128]{3,2,1,0:T(8,128)S(1)}, u32[]{:S(2)}, u32[]{:S(2)}) collective-permute-start(f32[2,192,8,128]{3,2,1,0:T(8,128)} %get-tuple-element.94), channel_id=1, source_target_pairs={{1,0},{2,1},{3,2},{4,3},{5,4},{6,5},{7,6},{8,7},{9,8},{10,9},{11,1... | collective-permute-start | bytes 4718600 | tf_op jit(solution)/shard_map/ppermute | solution.py:15
  373.7 84.9 %collective-permute-start.10 = (f32[2,192,8,128]{3,2,1,0:T(8,128)S(1)}, f32[2,192,8,128]{3,2,1,0:T(8,128)S(1)}, u32[]{:S(2)}, u32[]{:S(2)}) collective-permute-start(f32[2,192,8,128]{3,2,1,0:T(8,128)S(1)} %get-tuple-element.95), channel_id=1, source_target_pairs={{3,0},{4,1},{5,2},{6,3},{7,4},{8,5},{9,6},{10,7},{11,8},{12,9},{13... | collective-permute-start | bytes 4718600 | tf_op jit(solution)/shard_map/ppermute | solution.py:15
  394.8 63.8 %collective-permute-start.9 = (f32[2,192,8,128]{3,2,1,0:T(8,128)S(1)}, f32[2,192,8,128]{3,2,1,0:T(8,128)S(1)}, u32[]{:S(2)}, u32[]{:S(2)}) collective-permute-start(f32[2,192,8,128]{3,2,1,0:T(8,128)S(1)} %get-tuple-element.96), channel_id=1, source_target_pairs={{4,0},{5,1},{6,2},{7,3},{8,4},{9,5},{10,6},{11,7},{12,8},{13,9},{1... | collective-permute-start | bytes 4718600 | tf_op jit(solution)/shard_map/ppermute | solution.py:15
  403.3 55.3 %collective-permute-start.15 = (f32[2,192,8,128]{3,2,1,0:T(8,128)S(1)}, f32[2,192,8,128]{3,2,1,0:T(8,128)S(1)}, u32[]{:S(2)}, u32[]{:S(2)}) collective-permute-start(f32[2,192,8,128]{3,2,1,0:T(8,128)S(1)} %get-tuple-element.97), channel_id=1, source_target_pairs={{0,5},{1,6},{2,7},{3,8},{4,9},{5,10},{6,11},{7,12},{8,13},{9,14},{... | collective-permute-start | bytes 4718600 | tf_op jit(solution)/shard_map/ppermute | solution.py:15
  456.7 71.4 %collective-permute-start.14 = (f32[2,192,8,128]{3,2,1,0:T(8,128)S(1)}, f32[2,192,8,128]{3,2,1,0:T(8,128)S(1)}, u32[]{:S(2)}, u32[]{:S(2)}) collective-permute-start(f32[2,192,8,128]{3,2,1,0:T(8,128)S(1)} %get-tuple-element.98), channel_id=1, source_target_pairs={{0,4},{1,5},{2,6},{3,7},{4,8},{5,9},{6,10},{7,11},{8,12},{9,13},{1... | collective-permute-start | bytes 4718600 | tf_op jit(solution)/shard_map/ppermute | solution.py:15
  528.1 3.2 copy-start.1
where the time goes:
time: 533 us; the launch traced here: 531 us
  waiting for transfers between devices  198 us (37%)
  local copies, waits for them, and re-layouts  146 us (27%)
  other arithmetic  113 us (21%)
  starting transfers between devices  48.2 us (9%)
  matrix products  24 us (5%)
    ppermute x16, waiting for transfers between devices, passed_along(): lax.ppermute(value, axis, [(source, source + steps) for source in range(f...  198 us
    scatter-add x3, other arithmetic, one_tile(): bank_acc = bank_acc.at[:, slot_row].add(parts_both)  83.5 us
    ppermute x16, starting transfers between devices, passed_along(): lax.ppermute(value, axis, [(source, source + steps) for source in range(f...  48.2 us
    another operation x9, local copies, waits for them, and re-layouts, one_tile(): jnp.stack([part_keys, part_values]).reshape(2, list_len, row_width)  48.2 us
    another operation x3, other arithmetic, one_tile(): jnp.stack([part_keys, part_values]).reshape(2, list_len, row_width)  21.7 us
    while x1, local copies, waits for them, and re-layouts, on_device(): lax.scan(one_tile, bank_init, (query_tiles, grad_tiles, slots, valid))  19 us
    reshape x1, local copies, waits for them, and re-layouts, on_device(): bank_grad.reshape(2, len(BAND_OFFSETS), tok_dev, heads, head_dim)  15.2 us
    gather x3, local copies, waits for them, and re-layouts, one_tile(): jnp.take(bank, slot_row, axis=1)  12.5 us
  transfers between devices with their start and end apart: 16, of which 8 were waited for; matrix products, arithmetic and copies ran while one was open for 2% of the time, Pallas kernels for 0%

commit v1 on v0

v1 whole, which is shorter than its diff:
```python
import functools

import jax
import jax.numpy as jnp
from jax import lax
from jax.experimental import pallas as pl
from jax.experimental.pallas import tpu as pltpu
from jax.sharding import PartitionSpec as P

TILE = 64
ROWS = 4
MESH = pl.DeviceIdType.MESH
LOG2E = 1.4426950408889634
HIDE = -1e30
CENTRE = 4
KEYS, VALUES, QUERIES, GRADS = range(4)


def slot_of(frame_step, row_step):
    return (frame_step + 1) * 3 + row_step + 1


def dot(a, b, contract):
    return lax.dot_general(a, b, (((contract[0],), (contract[1],)), ((), ())), preferred_element_type=jnp.float32)


def kernel(devices, x_ref, kv_ref, out_ref, bank, stats, bias_q, bias_k, load_sem, send_sem, recv_sem, stat_send, stat_recv):
    heads, tok, dim = x_ref.shape[1:]
    cols = tok // TILE
    band = 9 * tok
    scale = dim ** -0.5
    me = lax.axis_index("seq")
    frame, row = me // ROWS, me % ROWS
    frames = devices // ROWS
    has_frame = {-1: frame > 0, 1: frame < frames - 1}
    has_row = {-1: row > 0, 1: row < ROWS - 1}
    crosses = {-1: row == 2, 1: row == 1}
    middle = (row == 1) | (row == 2)
    row_way = jnp.where(row == 1, 1, -1)

    def has(df, dr):
        cond = None
        if df:
            cond = has_frame[df]
        if dr:
            cond = has_row[dr] if cond is None else cond & has_row[dr]
        return cond

    around = [(df, dr) for df in (-1, 0, 1) for dr in (-1, 0, 1) if df or dr]

    load = pltpu.make_async_copy(x_ref, bank.at[:, :, CENTRE], load_sem)
    load.start()
    barrier = pltpu.get_barrier_semaphore()
    for df, dr in around:
        @pl.when(has(df, dr))
        def _():
            pl.semaphore_signal(barrier, inc=1, device_id={"seq": me + df * ROWS + dr}, device_id_type=MESH)
    frame_peers = jnp.where(has_frame[-1], 1, 0) + jnp.where(has_frame[1], 1, 0) + 1
    row_peers = jnp.where(has_row[-1], 1, 0) + jnp.where(has_row[1], 1, 0) + 1
    pl.semaphore_wait(barrier, frame_peers * row_peers - 1)

    def remote(g, h, src, dst, step, kind):
        c = g * heads + h
        return pltpu.make_async_remote_copy(
            src_ref=bank.at[pl.ds(2 * g, 2), h, src], dst_ref=bank.at[pl.ds(2 * g, 2), h, dst],
            send_sem=send_sem.at[kind, c], recv_sem=recv_sem.at[dst, c],
            device_id={"seq": me + step}, device_id_type=MESH)

    def wait_in(g, h, slot):
        c = g * heads + h
        part = bank.at[pl.ds(2 * g, 2), h, slot]
        pltpu.make_async_copy(part, part, recv_sem.at[slot, c]).wait()

    def frame_first(h):
        return h % 3 != 1

    def own_sends(g, h, act):
        for k, df in enumerate((-1, 1)):
            @pl.when(has_frame[df])
            def _():
                act(remote(g, h, CENTRE, slot_of(-df, 0), df * ROWS, k))
        for k, dr in enumerate((-1, 1)):
            @pl.when(has_row[dr])
            def _():
                act(remote(g, h, CENTRE, slot_of(0, -dr), dr, 2 + k))

    def later_sends(g, h, act, wait):
        kind = 4
        for df in (-1, 1):
            if wait:
                @pl.when(has_frame[df])
                def _():
                    wait_in(g, h, slot_of(df, 0))
            for dr in (-1, 1):
                @pl.when(has(df, dr) & (frame_first(h) | ~crosses[dr]))
                def _():
                    act(remote(g, h, slot_of(df, 0), slot_of(df, -dr), dr, kind))
                kind += 1
        if wait:
            @pl.when(middle & ~frame_first(h))
            def _():
                wait_in(g, h, CENTRE + row_way)
        for df in (-1, 1):
            @pl.when(has_frame[df] & middle & ~frame_first(h))
            def _():
                act(remote(g, h, CENTRE + row_way, (1 - df) * 3 + 1 + row_way, df * ROWS, kind))
            kind += 1

    def wait_rest(g, h):
        for dr in (-1, 1):
            @pl.when(has_row[dr] & (frame_first(h) | ~crosses[dr]))
            def _():
                wait_in(g, h, slot_of(0, dr))
        for df in (-1, 1):
            for dr in (-1, 1):
                @pl.when(has(df, dr))
                def _():
                    wait_in(g, h, slot_of(df, dr))

    def stat_copy(h, df, dr):
        dst = slot_of(-df, -dr)
        return pltpu.make_async_remote_copy(
            src_ref=stats.at[h, CENTRE], dst_ref=stats.at[h, dst],
            send_sem=stat_send.at[dst, h], recv_sem=stat_recv.at[dst, h],
            device_id={"seq": me + df * ROWS + dr}, device_id_type=MESH)

    def start(copy):
        copy.start()

    def wait_send(copy):
        copy.wait_send()

    load.wait()
    own_sends(0, 0, start)
    own_sends(0, 1, start)
    own_sends(1, 0, start)

    for df, dr in around:
        @pl.when(~has(df, dr))
        def _():
            slot = slot_of(df, dr)

            def clear(h, carry):
                for a in range(4):
                    bank[a, h, slot] = jnp.zeros((tok, dim), bank.dtype)
                stats[h, slot] = jnp.zeros(stats.shape[2:], stats.dtype)
                return carry

            lax.fori_loop(0, heads, clear, 0)

    tiles = kv_ref.shape[0]
    tile_ids = lax.broadcasted_iota(jnp.int32, (tiles, tiles), 1)
    listed = jnp.zeros((tiles, tiles), jnp.float32)
    for e in range(kv_ref.shape[1]):
        listed = jnp.where(kv_ref[:, e:e + 1] == tile_ids, 1.0, listed)
    lane = lax.broadcasted_iota(jnp.int32, (tiles, band), 1)
    slot_at = jnp.zeros_like(lane)
    for j in range(1, 9):
        slot_at += (lane >= j * tok).astype(jnp.int32)
    df_at = (lane >= 3 * tok).astype(jnp.int32) + (lane >= 6 * tok).astype(jnp.int32) - 1
    dr_at = slot_at - 3 * (df_at + 1) - 1
    col_at = lax.shift_right_logical(lane - slot_at * tok, 6)
    there = (frame + df_at >= 0) & (frame + df_at < frames) & (row + dr_at >= 0) & (row + dr_at < ROWS)
    tile_at = jnp.where(there, (me + df_at * ROWS + dr_at) * cols + col_at, -1)
    place = jnp.where(tile_at == lax.broadcasted_iota(jnp.int32, (tiles, band), 0), 1.0, 0.0)
    mine = jnp.where(
        lax.broadcasted_iota(jnp.int32, (8, tiles), 1) == me * cols + lax.broadcasted_iota(jnp.int32, (8, tiles), 0),
        1.0, 0.0)
    bias_q[...] = jnp.where(dot(dot(mine, listed, (1, 0)), place, (1, 0)) > 0.5, 0.0, HIDE)
    bias_k[...] = jnp.where(dot(dot(mine, listed, (1, 1)), place, (1, 0)) > 0.5, 0.0, HIDE)

    def rows_of(x, t):
        return x[t * TILE:(t + 1) * TILE]

    def queries_side(h):
        q, do = bank[QUERIES, h, CENTRE], bank[GRADS, h, CENTRE]
        k, v = bank[KEYS, h].reshape(band, dim), bank[VALUES, h].reshape(band, dim)
        s = dot(q, k, (1, 1))
        weights, tops, totals = [], [], []
        for t in range(cols):
            z = rows_of(s, t) * (scale * LOG2E) + bias_q[t:t + 1, :]
            top = jnp.max(z, axis=1, keepdims=True)
            w = jnp.exp2(z - top)
            weights.append(w)
            tops.append(top)
            totals.append(jnp.sum(w, axis=1, keepdims=True))
        w = jnp.concatenate(weights, axis=0)
        top, total = jnp.concatenate(tops, axis=0), jnp.concatenate(totals, axis=0)
        inv = 1.0 / total
        out = (dot(w.astype(jnp.bfloat16), v, (1, 0)) * inv).astype(jnp.bfloat16)
        out_ref[0, h] = out
        delta = jnp.sum(do.astype(jnp.float32) * out.astype(jnp.float32), axis=1, keepdims=True)
        dw = dot(do, v, (1, 1))
        ds = (w * (dw - delta) * (inv * scale)).astype(jnp.bfloat16)
        out_ref[1, h] = dot(ds, k, (1, 0)).astype(jnp.bfloat16)
        lse = top + jnp.log(total) * LOG2E
        wide = jnp.where(lax.broadcasted_iota(jnp.int32, (tok, 128), 1) == 0, lse, delta)
        turned = jnp.transpose(wide)
        stats[h, CENTRE, :, 0:tok] = turned[0:8]

    def keys_side(h):
        k, v = bank[KEYS, h, CENTRE], bank[VALUES, h, CENTRE]
        q, do = bank[QUERIES, h].reshape(band, dim), bank[GRADS, h].reshape(band, dim)
        s = dot(k, q, (1, 1))
        st = jnp.concatenate([stats[h, j, :, 0:tok] for j in range(9)], axis=1)
        lse, delta = st[0:1], st[1:2]
        w = jnp.concatenate(
            [jnp.exp2(rows_of(s, t) * (scale * LOG2E) + (bias_k[t:t + 1, :] - lse)) for t in range(cols)], axis=0)
        out_ref[3, h] = dot(w.astype(jnp.bfloat16), do, (1, 0)).astype(jnp.bfloat16)
        dw = dot(v, do, (1, 1))
        ds = (w * ((dw - delta) * scale)).astype(jnp.bfloat16)
        out_ref[2, h] = dot(ds, q, (1, 0)).astype(jnp.bfloat16)

    later_sends(0, 0, start, True)

    def step(i, carry):
        @pl.when(i + 2 < heads)
        def _():
            own_sends(0, i + 2, start)

        @pl.when(i + 1 < heads)
        def _():
            own_sends(1, i + 1, start)
            later_sends(0, i + 1, start, True)

        @pl.when(i < heads)
        def _():
            later_sends(1, i, start, True)
            wait_rest(0, i)
            queries_side(i)
            for df, dr in around:
                @pl.when(has(df, dr))
                def _():
                    stat_copy(i, df, dr).start()

        @pl.when(i >= 1)
        def _():
            wait_rest(1, i - 1)
            for df, dr in around:
                @pl.when(has(df, dr))
                def _():
                    slot = slot_of(df, dr)
                    part = stats.at[i - 1, slot]
                    pltpu.make_async_copy(part, part, stat_recv.at[slot, i - 1]).wait()
            keys_side(i - 1)

        return carry

    lax.fori_loop(0, heads + 1, step, 0)

    def finish(h, carry):
        for g in range(2):
            own_sends(g, h, wait_send)
            later_sends(g, h, wait_send, False)
        for df, dr in around:
            @pl.when(has(df, dr))
            def _():
                stat_copy(h, df, dr).wait_send()
        return carry

    lax.fori_loop(0, heads, finish, 0)


def on_device(devices, queries, key_rows, value_rows, grad_out, kv_tiles, counts):
    tok, heads, dim = queries.shape
    x = jnp.stack([key_rows, value_rows, queries, grad_out]).transpose(0, 2, 1, 3)
    out = pl.pallas_call(
        functools.partial(kernel, devices),
        out_shape=jax.ShapeDtypeStruct((4, heads, tok, dim), jnp.bfloat16),
        in_specs=[pl.BlockSpec(memory_space=pl.ANY), pl.BlockSpec(memory_space=pltpu.VMEM)],
        out_specs=pl.BlockSpec(memory_space=pltpu.VMEM),
        scratch_shapes=[
            pltpu.VMEM((4, heads, 9, tok, dim), jnp.bfloat16),
            pltpu.VMEM((heads, 9, 8, 256), jnp.float32),
            pltpu.VMEM((8, 9 * tok), jnp.float32),
            pltpu.VMEM((8, 9 * tok), jnp.float32),
            pltpu.SemaphoreType.DMA,
            pltpu.SemaphoreType.DMA((10, 2 * heads)),
            pltpu.SemaphoreType.DMA((9, 2 * heads)),
            pltpu.SemaphoreType.DMA((9, heads)),
            pltpu.SemaphoreType.DMA((9, heads)),
        ],
        compiler_params=pltpu.CompilerParams(collective_id=0, has_side_effects=True, vmem_limit_bytes=56 * 2**20),
    )(x, kv_tiles)
    out = out.transpose(0, 2, 1, 3)
    return (out[0], out[1], out[2], out[3])


def solution(mesh):
    rows = P(("parts", "seq"), None, None)
    return jax.shard_map(
        functools.partial(on_device, mesh.shape["seq"]),
        mesh=mesh,
        in_specs=(rows, rows, rows, rows, P("parts", None), P("parts")),
        out_specs=(rows, rows, rows, rows),
        check_vma=False,
    )
```

time: 533 us -> 70.3 us (0.13)
  the two profiles are of different devices: /device:TPU:22 before, /device:TPU:1 now
where the time goes in v1:
time: 70.3 us; the launch traced here: 70 us
  Pallas kernels  59.6 us (85%)
  local copies, waits for them, and re-layouts  8.33 us (12%)
  other arithmetic  1.36 us (2%)
    pallas_call x1, Pallas kernels, on_device(): pl.pallas_call(functools.partial(kernel, devices), out_shape=jax.ShapeDty...  59.6 us
    unnamed x9, local copies, waits for them, and re-layouts  5.48 us
    squeeze x1, local copies, waits for them, and re-layouts, on_device(): return (out[0], out[1], out[2], out[3])  1.46 us

profile of v1, /device:TPU:1, one launch (start us, length us, event | category | flops | bytes accessed | tf_op | source)
XLA Modules:
  0.0 70.0 jit_solution(6198059080601295445)
XLA Ops:
  0.6 0.0 copy-start
  0.6 0.0 copy-start.1
  0.7 1.5 %copy.13.kv_ref = s32[48,12]{1,0:T(8,128)} copy(s32[48,12]{0,1:T(8,128)} %param.10) | data formatting | bytes 4608 | tf_op args[4]
  2.1 1.3 %copy_bitcast_fusion = (bf16[1,192,8,128]{3,1,2,0:T(8,128)(2,1)S(1)}, bf16[1,192,8,128]{3,1,2,0:T(8,128)(2,1)S(1)}) fusion(bf16[192,8,128]{2,1,0:T(8,128)(2,1)} %param.9, bf16[192,8,128]{2,1,0:T(8,128)(2,1)} %param.6), kind=kLoop, calls=%fused_computation.5 | loop fusion | bytes 1572864 | tf_op jit(solution)/shard_map/stack | solution.py:266
  3.4 0.0 copy-done
  3.4 0.0 copy-done.1
  3.4 0.1 copy_bitcast_fusion.2
  3.5 1.4 %maximum_bitcast_fusion.x_ref = bf16[4,8,192,128]{3,2,1,0:T(8,128)(2,1)} fusion(bf16[1,192,8,128]{3,1,2,0:T(8,128)(2,1)S(1)} %get-tuple-element.12, bf16[1,192,8,128]{3,1,2,0:T(8,128)(2,1)S(1)} %get-tuple-element.13, bf16[1,192,8,128]{3,1,2,0:T(8,128)(2,1)S(1)} %get-tuple-element.14, bf16[1,192,8,128]{3,1,2,0:T(8,128)(2,1)S(1)} %get-tuple-element.15), kind=kLoop, calls=%fused_computation | loop fusion | flops 2359296 | bytes 3145728 | tf_op jit(solution)/shard_map/transpose | solution.py:266
  4.9 59.6 %shard_map.84 = bf16[4,8,192,128]{3,2,1,0:T(8,128)(2,1)} custom-call(bf16[4,8,192,128]{3,2,1,0:T(8,128)(2,1)} %maximum_bitcast_fusion.x_ref, s32[48,12]{1,0:T(8,128)} %copy.13.kv_ref), custom_call_target="tpu_custom_call" | custom-call | tf_op jit(solution)/shard_map/pallas_call | solution.py:267
  64.5 1.5 %slice_bitcast_fusion = (bf16[192,8,128]{2,0,1:T(8,128)(2,1)S(1)}, bf16[192,8,128]{2,0,1:T(8,128)(2,1)S(1)}, bf16[192,8,128]{2,0,1:T(8,128)(2,1)S(1)}, bf16[192,8,128]{2,0,1:T(8,128)(2,1)S(1)}) fusion(bf16[4,192,8,128]{3,1,2,0:T(8,128)(2,1)} %bitcast.19), kind=kLoop, calls=%fused_computation.1 | loop fusion | bytes 3145728 | tf_op jit(solution)/shard_map/squeeze | solution.py:286
  66.0 1.0 %copy.17 = bf16[192,8,128]{2,1,0:T(8,128)(2,1)} copy(bf16[192,8,128]{2,0,1:T(8,128)(2,1)S(1)} %get-tuple-element.8) | data formatting | bytes 786432
  67.0 1.0 %copy.16 = bf16[192,8,128]{2,1,0:T(8,128)(2,1)} copy(bf16[192,8,128]{2,0,1:T(8,128)(2,1)S(1)} %get-tuple-element.9) | data formatting | bytes 786432
  68.0 1.0 %copy.15 = bf16[192,8,128]{2,1,0:T(8,128)(2,1)} copy(bf16[192,8,128]{2,0,1:T(8,128)(2,1)S(1)} %get-tuple-element.10) | data formatting | bytes 786432
  69.0 1.0 %copy.14 = bf16[192,8,128]{2,1,0:T(8,128)(2,1)} copy(bf16[192,8,128]{2,0,1:T(8,128)(2,1)S(1)} %get-tuple-element.11) | data formatting | bytes 786432
Async XLA Ops:
  0.6 2.7 %copy-start = (bf16[192,8,128]{2,1,0:T(8,128)(2,1)S(1)}, bf16[192,8,128]{2,1,0:T(8,128)(2,1)}, u32[]{:S(2)}) copy-start(bf16[192,8,128]{2,1,0:T(8,128)(2,1)} %param.8) | copy-start | bytes 1179652
  0.6 2.7 %copy-start.1 = (bf16[192,8,128]{2,1,0:T(8,128)(2,1)S(1)}, bf16[192,8,128]{2,1,0:T(8,128)(2,1)}, u32[]{:S(2)}) copy-start(bf16[192,8,128]{2,1,0:T(8,128)(2,1)} %param.7) | copy-start | bytes 1179652

commit v2 on v1

--- a/solution.py
+++ b/solution.py
@@ -13,6 +13,7 @@
 LOG2E = 1.4426950408889634
 HIDE = -1e30
 CENTRE = 4
+OWN_AHEAD, PASS_AHEAD, LAG = 4, 2, 2
 KEYS, VALUES, QUERIES, GRADS = range(4)
 
 
@@ -24,8 +25,8 @@
     return lax.dot_general(a, b, (((contract[0],), (contract[1],)), ((), ())), preferred_element_type=jnp.float32)
 
 
-def kernel(devices, x_ref, kv_ref, out_ref, bank, stats, bias_q, bias_k, load_sem, send_sem, recv_sem, stat_send, stat_recv):
-    heads, tok, dim = x_ref.shape[1:]
+def kernel(devices, k_ref, v_ref, q_ref, do_ref, kv_ref, out_ref, bank, stats, bias_q, bias_k, send_sem, recv_sem, stat_send, stat_recv):
+    tok, heads, dim = q_ref.shape
     cols = tok // TILE
     band = 9 * tok
     scale = dim ** -0.5
@@ -48,8 +49,6 @@
 
     around = [(df, dr) for df in (-1, 0, 1) for dr in (-1, 0, 1) if df or dr]
 
-    load = pltpu.make_async_copy(x_ref, bank.at[:, :, CENTRE], load_sem)
-    load.start()
     barrier = pltpu.get_barrier_semaphore()
     for df, dr in around:
         @pl.when(has(df, dr))
@@ -57,6 +56,8 @@
             pl.semaphore_signal(barrier, inc=1, device_id={"seq": me + df * ROWS + dr}, device_id_type=MESH)
     frame_peers = jnp.where(has_frame[-1], 1, 0) + jnp.where(has_frame[1], 1, 0) + 1
     row_peers = jnp.where(has_row[-1], 1, 0) + jnp.where(has_row[1], 1, 0) + 1
+    for a, ref in enumerate((k_ref, v_ref, q_ref, do_ref)):
+        bank[a, :, CENTRE] = jnp.transpose(ref[...], (1, 0, 2))
     pl.semaphore_wait(barrier, frame_peers * row_peers - 1)
 
     def remote(g, h, src, dst, step, kind):
@@ -130,10 +131,10 @@
     def wait_send(copy):
         copy.wait_send()
 
-    load.wait()
-    own_sends(0, 0, start)
-    own_sends(0, 1, start)
-    own_sends(1, 0, start)
+    for lead in range(OWN_AHEAD - PASS_AHEAD):
+        own_sends(0, lead, start)
+        if lead >= LAG:
+            own_sends(1, lead - LAG, start)
 
     for df, dr in around:
         @pl.when(~has(df, dr))
@@ -148,11 +149,11 @@
 
             lax.fori_loop(0, heads, clear, 0)
 
-    tiles = kv_ref.shape[0]
-    tile_ids = lax.broadcasted_iota(jnp.int32, (tiles, tiles), 1)
+    tiles = kv_ref.shape[1]
+    tile_ids = lax.broadcasted_iota(jnp.int32, (tiles, tiles), 0)
     listed = jnp.zeros((tiles, tiles), jnp.float32)
-    for e in range(kv_ref.shape[1]):
-        listed = jnp.where(kv_ref[:, e:e + 1] == tile_ids, 1.0, listed)
+    for e in range(kv_ref.shape[0]):
+        listed = jnp.where(kv_ref[e:e + 1, :] == tile_ids, 1.0, listed)
     lane = lax.broadcasted_iota(jnp.int32, (tiles, band), 1)
     slot_at = jnp.zeros_like(lane)
     for j in range(1, 9):
@@ -166,8 +167,8 @@
     mine = jnp.where(
         lax.broadcasted_iota(jnp.int32, (8, tiles), 1) == me * cols + lax.broadcasted_iota(jnp.int32, (8, tiles), 0),
         1.0, 0.0)
-    bias_q[...] = jnp.where(dot(dot(mine, listed, (1, 0)), place, (1, 0)) > 0.5, 0.0, HIDE)
-    bias_k[...] = jnp.where(dot(dot(mine, listed, (1, 1)), place, (1, 0)) > 0.5, 0.0, HIDE)
+    bias_q[...] = jnp.where(dot(dot(mine, listed, (1, 1)), place, (1, 0)) > 0.5, 0.0, HIDE)
+    bias_k[...] = jnp.where(dot(dot(mine, listed, (1, 0)), place, (1, 0)) > 0.5, 0.0, HIDE)
 
     def rows_of(x, t):
         return x[t * TILE:(t + 1) * TILE]
@@ -211,21 +212,36 @@
         ds = (w * ((dw - delta) * scale)).astype(jnp.bfloat16)
         out_ref[2, h] = dot(ds, q, (1, 0)).astype(jnp.bfloat16)
 
-    later_sends(0, 0, start, True)
-
-    def step(i, carry):
-        @pl.when(i + 2 < heads)
-        def _():
-            own_sends(0, i + 2, start)
-
-        @pl.when(i + 1 < heads)
-        def _():
-            own_sends(1, i + 1, start)
-            later_sends(0, i + 1, start, True)
-
-        @pl.when(i < heads)
-        def _():
-            later_sends(1, i, start, True)
+    def step(t, carry):
+        def at(lag):
+            h = t - lag
+            if lag > 0:
+                return h, (h >= 0) & (h < heads)
+            return h, h < heads
+
+        h_own, turn = at(PASS_AHEAD - OWN_AHEAD)
+        @pl.when(turn)
+        def _():
+            own_sends(0, h_own, start)
+
+        h_own_late, turn = at(PASS_AHEAD - OWN_AHEAD + LAG)
+        @pl.when(turn)
+        def _():
+            own_sends(1, h_own_late, start)
+
+        h_pass, turn = at(0)
+        @pl.when(turn)
+        def _():
+            later_sends(0, h_pass, start, True)
+
+        h_pass_late, turn = at(LAG)
+        @pl.when(turn)
+        def _():
+            later_sends(1, h_pass_late, start, True)
+
+        i, turn = at(PASS_AHEAD)
+        @pl.when(turn)
+        def _():
             wait_rest(0, i)
             queries_side(i)
             for df, dr in around:
@@ -233,20 +249,21 @@
                 def _():
                     stat_copy(i, df, dr).start()
 
-        @pl.when(i >= 1)
-        def _():
-            wait_rest(1, i - 1)
+        h, turn = at(PASS_AHEAD + LAG)
+        @pl.when(turn)
+        def _():
+            wait_rest(1, h)
             for df, dr in around:
                 @pl.when(has(df, dr))
                 def _():
                     slot = slot_of(df, dr)
-                    part = stats.at[i - 1, slot]
-                    pltpu.make_async_copy(part, part, stat_recv.at[slot, i - 1]).wait()
-            keys_side(i - 1)
+                    part = stats.at[h, slot]
+                    pltpu.make_async_copy(part, part, stat_recv.at[slot, h]).wait()
+            keys_side(h)
 
         return carry
 
-    lax.fori_loop(0, heads + 1, step, 0)
+    lax.fori_loop(0, heads + LAG + PASS_AHEAD, step, 0)
 
     def finish(h, carry):
         for g in range(2):
@@ -261,29 +278,36 @@
     lax.fori_loop(0, heads, finish, 0)
 
 
+def by_token(in_ref, *out_refs):
+    for a, ref in enumerate(out_refs):
+        ref[...] = jnp.transpose(in_ref[a], (1, 0, 2))
+
+
 def on_device(devices, queries, key_rows, value_rows, grad_out, kv_tiles, counts):
     tok, heads, dim = queries.shape
-    x = jnp.stack([key_rows, value_rows, queries, grad_out]).transpose(0, 2, 1, 3)
     out = pl.pallas_call(
         functools.partial(kernel, devices),
         out_shape=jax.ShapeDtypeStruct((4, heads, tok, dim), jnp.bfloat16),
-        in_specs=[pl.BlockSpec(memory_space=pl.ANY), pl.BlockSpec(memory_space=pltpu.VMEM)],
+        in_specs=[pl.BlockSpec(memory_space=pltpu.VMEM)] * 5,
         out_specs=pl.BlockSpec(memory_space=pltpu.VMEM),
         scratch_shapes=[
             pltpu.VMEM((4, heads, 9, tok, dim), jnp.bfloat16),
             pltpu.VMEM((heads, 9, 8, 256), jnp.float32),
             pltpu.VMEM((8, 9 * tok), jnp.float32),
             pltpu.VMEM((8, 9 * tok), jnp.float32),
-            pltpu.SemaphoreType.DMA,
             pltpu.SemaphoreType.DMA((10, 2 * heads)),
             pltpu.SemaphoreType.DMA((9, 2 * heads)),
             pltpu.SemaphoreType.DMA((9, heads)),
             pltpu.SemaphoreType.DMA((9, heads)),
         ],
         compiler_params=pltpu.CompilerParams(collective_id=0, has_side_effects=True, vmem_limit_bytes=56 * 2**20),
-    )(x, kv_tiles)
-    out = out.transpose(0, 2, 1, 3)
-    return (out[0], out[1], out[2], out[3])
+    )(key_rows, value_rows, queries, grad_out, kv_tiles.T)
+    return tuple(pl.pallas_call(
+        by_token,
+        out_shape=[jax.ShapeDtypeStruct(queries.shape, queries.dtype)] * 4,
+        in_specs=[pl.BlockSpec(memory_space=pltpu.VMEM)],
+        out_specs=[pl.BlockSpec(memory_space=pltpu.VMEM)] * 4,
+    )(out))
 
 
 def solution(mesh):

time: 70.3 us -> 63.4 us (0.902)
  local copies, waits for them, and re-layouts: 8.33 us -> 0 us
  Pallas kernels: 59.6 us -> 62.6 us
  other arithmetic: 1.36 us -> 0 us
    unnamed x9 -> x0, local copies, waits for them, and re-layouts: 5.48 us -> none
    pallas_call x0 -> x1, Pallas kernels: none -> 2.6 us  [on_device(): pl.pallas_call(by_token, out_shape=[jax.ShapeDtypeStruct(queries.shape, q...]
    squeeze x1 -> x0, local copies, waits for them, and re-layouts: 1.46 us -> none  [on_device(): return (out[0], out[1], out[2], out[3])]
    another operation x2 -> x0, local copies, waits for them, and re-layouts: 1.39 us -> none  [on_device(): jnp.stack([key_rows, value_rows, queries, grad_out]).transpose(0, 2, 1, 3)]
    transpose x1 -> x0, other arithmetic: 1.36 us -> none  [on_device(): jnp.stack([key_rows, value_rows, queries, grad_out]).transpose(0, 2, 1, 3)]
where the time goes in v2:
time: 63.4 us; the launch traced here: 63.2 us
  Pallas kernels  62.6 us (99%)
  between operations  0.64 us (1%)
    pallas_call x1, Pallas kernels, on_device(): pl.pallas_call(functools.partial(kernel, devices), out_shape=jax.ShapeDty...  60 us
    pallas_call x1, Pallas kernels, on_device(): pl.pallas_call(by_token, out_shape=[jax.ShapeDtypeStruct(queries.shape, q...  2.6 us

profile of v2, /device:TPU:1, one launch (start us, length us, event | category | flops | bytes accessed | tf_op | source)
XLA Modules:
  0.0 63.2 jit_solution(8761161343420209473)
XLA Ops:
  0.6 60.0 %shard_map.84.in_ref = bf16[4,8,192,128]{3,2,1,0:T(8,128)(2,1)} custom-call(bf16[192,8,128]{2,1,0:T(8,128)(2,1)} %k_ref.1, bf16[192,8,128]{2,1,0:T(8,128)(2,1)} %v_ref.1, bf16[192,8,128]{2,1,0:T(8,128)(2,1)} %q_ref.1, bf16[192,8,128]{2,1,0:T(8,128)(2,1)} %do_ref.1, s32[12,48]{1,0:T(8,128)} %bitcast.1), custom_call_target="tpu_custom_call" | custom-call | tf_op jit(solution)/shard_map/pallas_call | solution.py:288
  60.6 2.6 %shard_map.85 = (bf16[192,8,128]{2,1,0:T(8,128)(2,1)}, bf16[192,8,128]{2,1,0:T(8,128)(2,1)}, bf16[192,8,128]{2,1,0:T(8,128)(2,1)}, bf16[192,8,128]{2,1,0:T(8,128)(2,1)}) custom-call(bf16[4,8,192,128]{3,2,1,0:T(8,128)(2,1)} %shard_map.84.in_ref), custom_call_target="tpu_custom_call" | custom-call | tf_op jit(solution)/shard_map/pallas_call | solution.py:305

commit v3 on v2

--- a/solution.py
+++ b/solution.py
@@ -56,8 +56,8 @@
             pl.semaphore_signal(barrier, inc=1, device_id={"seq": me + df * ROWS + dr}, device_id_type=MESH)
     frame_peers = jnp.where(has_frame[-1], 1, 0) + jnp.where(has_frame[1], 1, 0) + 1
     row_peers = jnp.where(has_row[-1], 1, 0) + jnp.where(has_row[1], 1, 0) + 1
-    for a, ref in enumerate((k_ref, v_ref, q_ref, do_ref)):
-        bank[a, :, CENTRE] = jnp.transpose(ref[...], (1, 0, 2))
+    bank[KEYS, :, CENTRE] = jnp.transpose(k_ref[...], (1, 0, 2))
+    bank[VALUES, :, CENTRE] = jnp.transpose(v_ref[...], (1, 0, 2))
     pl.semaphore_wait(barrier, frame_peers * row_peers - 1)
 
     def remote(g, h, src, dst, step, kind):
@@ -73,7 +73,7 @@
         pltpu.make_async_copy(part, part, recv_sem.at[slot, c]).wait()
 
     def frame_first(h):
-        return h % 3 != 1
+        return (h % 2 == 0) | (h < 2)
 
     def own_sends(g, h, act):
         for k, df in enumerate((-1, 1)):
@@ -81,7 +81,13 @@
             def _():
                 act(remote(g, h, CENTRE, slot_of(-df, 0), df * ROWS, k))
         for k, dr in enumerate((-1, 1)):
-            @pl.when(has_row[dr])
+            @pl.when(has_row[dr] & (frame_first(h) | ~crosses[dr]))
+            def _():
+                act(remote(g, h, CENTRE, slot_of(0, -dr), dr, 2 + k))
+
+    def crossing_sends(g, h, act):
+        for k, dr in enumerate((-1, 1)):
+            @pl.when(crosses[dr] & ~frame_first(h))
             def _():
                 act(remote(g, h, CENTRE, slot_of(0, -dr), dr, 2 + k))
 
@@ -133,8 +139,15 @@
 
     for lead in range(OWN_AHEAD - PASS_AHEAD):
         own_sends(0, lead, start)
-        if lead >= LAG:
-            own_sends(1, lead - LAG, start)
+    bank[QUERIES, :, CENTRE] = jnp.transpose(q_ref[...], (1, 0, 2))
+    bank[GRADS, :, CENTRE] = jnp.transpose(do_ref[...], (1, 0, 2))
+
+    def cross(h, carry):
+        crossing_sends(0, h, start)
+        crossing_sends(1, h, start)
+        return carry
+
+    lax.fori_loop(0, heads, cross, 0)
 
     for df, dr in around:
         @pl.when(~has(df, dr))
@@ -197,7 +210,7 @@
         lse = top + jnp.log(total) * LOG2E
         wide = jnp.where(lax.broadcasted_iota(jnp.int32, (tok, 128), 1) == 0, lse, delta)
         turned = jnp.transpose(wide)
-        stats[h, CENTRE, :, 0:tok] = turned[0:8]
+        stats[h, CENTRE, :, 0:tok] = turned[0:2]
 
     def keys_side(h):
         k, v = bank[KEYS, h, CENTRE], bank[VALUES, h, CENTRE]
@@ -268,6 +281,7 @@
     def finish(h, carry):
         for g in range(2):
             own_sends(g, h, wait_send)
+            crossing_sends(g, h, wait_send)
             later_sends(g, h, wait_send, False)
         for df, dr in around:
             @pl.when(has(df, dr))
@@ -292,7 +306,7 @@
         out_specs=pl.BlockSpec(memory_space=pltpu.VMEM),
         scratch_shapes=[
             pltpu.VMEM((4, heads, 9, tok, dim), jnp.bfloat16),
-            pltpu.VMEM((heads, 9, 8, 256), jnp.float32),
+            pltpu.VMEM((heads, 9, 2, 256), jnp.float32),
             pltpu.VMEM((8, 9 * tok), jnp.float32),
             pltpu.VMEM((8, 9 * tok), jnp.float32),
             pltpu.SemaphoreType.DMA((10, 2 * heads)),

time: 63.4 us -> 61.2 us (0.965)
  Pallas kernels: 62.6 us -> 60.3 us
    pallas_call x1, Pallas kernels: 60 us -> 57.7 us  [on_device(): pl.pallas_call(functools.partial(kernel, devices), out_shape=jax.ShapeDty...]
where the time goes in v3:
time: 61.2 us; the launch traced here: 61 us
  Pallas kernels  60.3 us (99%)
  between operations  0.64 us (1%)
    pallas_call x1, Pallas kernels, on_device(): pl.pallas_call(functools.partial(kernel, devices), out_shape=jax.ShapeDty...  57.7 us
    pallas_call x1, Pallas kernels, on_device(): pl.pallas_call(by_token, out_shape=[jax.ShapeDtypeStruct(queries.shape, q...  2.6 us

profile of v3, /device:TPU:1, one launch (start us, length us, event | category | flops | bytes accessed | tf_op | source)
XLA Modules:
  0.0 61.0 jit_solution(15519903431710145940)
XLA Ops:
  0.6 57.7 %shard_map.84.in_ref = bf16[4,8,192,128]{3,2,1,0:T(8,128)(2,1)} custom-call(bf16[192,8,128]{2,1,0:T(8,128)(2,1)} %k_ref.1, bf16[192,8,128]{2,1,0:T(8,128)(2,1)} %v_ref.1, bf16[192,8,128]{2,1,0:T(8,128)(2,1)} %q_ref.1, bf16[192,8,128]{2,1,0:T(8,128)(2,1)} %do_ref.1, s32[12,48]{1,0:T(8,128)} %bitcast.1), custom_call_target="tpu_custom_call" | custom-call | tf_op jit(solution)/shard_map/pallas_call | solution.py:302
  58.4 2.6 %shard_map.85 = (bf16[192,8,128]{2,1,0:T(8,128)(2,1)}, bf16[192,8,128]{2,1,0:T(8,128)(2,1)}, bf16[192,8,128]{2,1,0:T(8,128)(2,1)}, bf16[192,8,128]{2,1,0:T(8,128)(2,1)}) custom-call(bf16[4,8,192,128]{3,2,1,0:T(8,128)(2,1)} %shard_map.84.in_ref), custom_call_target="tpu_custom_call" | custom-call | tf_op jit(solution)/shard_map/pallas_call | solution.py:319

commit v4 on v3

--- a/solution.py
+++ b/solution.py
@@ -232,6 +232,16 @@
                 return h, (h >= 0) & (h < heads)
             return h, h < heads
 
+        h_pass, turn = at(0)
+        @pl.when(turn)
+        def _():
+            later_sends(0, h_pass, start, True)
+
+        h_pass_late, turn = at(LAG)
+        @pl.when(turn)
+        def _():
+            later_sends(1, h_pass_late, start, True)
+
         h_own, turn = at(PASS_AHEAD - OWN_AHEAD)
         @pl.when(turn)
         def _():
@@ -241,16 +251,6 @@
         @pl.when(turn)
         def _():
             own_sends(1, h_own_late, start)
-
-        h_pass, turn = at(0)
-        @pl.when(turn)
-        def _():
-            later_sends(0, h_pass, start, True)
-
-        h_pass_late, turn = at(LAG)
-        @pl.when(turn)
-        def _():
-            later_sends(1, h_pass_late, start, True)
 
         i, turn = at(PASS_AHEAD)
         @pl.when(turn)

time: 61.2 us -> 61.9 us (1.011)
  Pallas kernels: 60.3 us -> 61.1 us
    pallas_call x1, Pallas kernels: 57.7 us -> 58.5 us  [on_device(): pl.pallas_call(functools.partial(kernel, devices), out_shape=jax.ShapeDty...]
where the time goes in v4:
time: 61.9 us; the launch traced here: 61.8 us
  Pallas kernels  61.1 us (99%)
  between operations  0.64 us (1%)
    pallas_call x1, Pallas kernels, on_device(): pl.pallas_call(functools.partial(kernel, devices), out_shape=jax.ShapeDty...  58.5 us
    pallas_call x1, Pallas kernels, on_device(): pl.pallas_call(by_token, out_shape=[jax.ShapeDtypeStruct(queries.shape, q...  2.6 us

profile of v4, /device:TPU:1, one launch (start us, length us, event | category | flops | bytes accessed | tf_op | source)
XLA Modules:
  0.0 61.8 jit_solution(15554424225419464039)
XLA Ops:
  0.6 58.5 %shard_map.84.in_ref = bf16[4,8,192,128]{3,2,1,0:T(8,128)(2,1)} custom-call(bf16[192,8,128]{2,1,0:T(8,128)(2,1)} %k_ref.1, bf16[192,8,128]{2,1,0:T(8,128)(2,1)} %v_ref.1, bf16[192,8,128]{2,1,0:T(8,128)(2,1)} %q_ref.1, bf16[192,8,128]{2,1,0:T(8,128)(2,1)} %do_ref.1, s32[12,48]{1,0:T(8,128)} %bitcast.1), custom_call_target="tpu_custom_call" | custom-call | tf_op jit(solution)/shard_map/pallas_call | solution.py:302
  59.2 2.6 %shard_map.85 = (bf16[192,8,128]{2,1,0:T(8,128)(2,1)}, bf16[192,8,128]{2,1,0:T(8,128)(2,1)}, bf16[192,8,128]{2,1,0:T(8,128)(2,1)}, bf16[192,8,128]{2,1,0:T(8,128)(2,1)}) custom-call(bf16[4,8,192,128]{3,2,1,0:T(8,128)(2,1)} %shard_map.84.in_ref), custom_call_target="tpu_custom_call" | custom-call | tf_op jit(solution)/shard_map/pallas_call | solution.py:319
